TPU v7x, 256 devices: a whole 4x4x8 slice. The times are simulated.
256 devices in a mesh: batch: 32 (over y_lo, z, core), tensor: 8 (over x, y_hi).
Axes of the slice: x: 4, y: 4 (y_hi: 2, y_lo: 2; y = y_hi * 2 + y_lo), z: 8, core: 2. Of those that a mesh axis runs over, the one named last changes fastest.
Arguments:
- queries: bfloat16 [128, 8192], P('batch', 'tensor'), may hold values from -80 to 80
- fresh_key_heads: bfloat16 [128, 1024], P('batch', 'tensor'), may hold values from -6 to 6
- fresh_value_heads: bfloat16 [128, 1024], P('batch', 'tensor'), may hold values from -6 to 6
- cached_keys: bfloat16 [128, 8, 4096, 128], P('batch', 'tensor'), may hold values from -6 to 6
- value_cache_rows: bfloat16 [128, 8, 4096, 128], P('batch', 'tensor'), may hold values from -6 to 6
- lengths: int32 [128], P('batch'), may hold values from 2 to 4096, as said below
- residual: bfloat16 [128, 5120], P('batch', 'tensor'), may hold values from -6 to 6
- sectioned_rows: bfloat16 [32, 256, 5120], P('batch', 'tensor'), may hold values from -0.5 to 0.5
- owners: int32 [32], replicated, may hold values from 0 to 31, each once
- norm_gain: bfloat16 [5120], P('tensor'), may hold values from 0.5 to 1.5
Outputs:
- updated_stream: bfloat16 [128, 5120], P('batch', 'tensor')
- normed_stream: bfloat16 [128, 5120], P('batch', 'tensor')
Inputs may be any that keep to these rules, and one draw needn't show every extreme that they name: `lengths`: every sequence has at least two valid positions; some sequence fills all 4096. `owners`: each batch index owns exactly one piece.
All inputs are finite; a program needn't handle non-finite values.
Results may differ from a plain program's by a relative error of at most 0.018.
Values may be sent and summed in bfloat16 or wider, within the bound.
A program may use at most 64 MiB of HBM per device.

v0:
```python
import jax
import jax.numpy as jnp
from jax import lax
from jax.sharding import PartitionSpec as P

D = 5120
QUERY_HEADS = 64
KEY_VALUE_HEADS = 8
HEAD_SIZE = 128


def local(
    queries,
    fresh_key_heads,
    fresh_value_heads,
    cached_keys,
    value_cache_rows,
    lengths,
    residual,
    sectioned_rows,
    owners,
    norm_gain,
):
    seqs_here = queries.shape[0]
    heads_kv = cached_keys.shape[1]
    span = cached_keys.shape[2]
    head_group = QUERY_HEADS // KEY_VALUE_HEADS
    score_scale = HEAD_SIZE ** (-0.5)
    head_count = queries.reshape(seqs_here, heads_kv, head_group, HEAD_SIZE)
    scores = (
        jnp.einsum("skgd,skld->skgl", head_count, cached_keys, preferred_element_type=jnp.float32)
        * score_scale
    )
    valid = jnp.arange(span)[None, :] < lengths[:, None]
    scores = jnp.where(valid[:, None, None, :], scores, -1e30)
    own_piece = (
        jnp.einsum(
            "skgd,skd->skg",
            head_count,
            fresh_key_heads.reshape(seqs_here, heads_kv, HEAD_SIZE),
            preferred_element_type=jnp.float32,
        )
        * score_scale
    )
    top = jnp.maximum(jnp.max(scores, axis=-1), own_piece)
    probs = jnp.exp(scores - top[..., None])
    own_probability = jnp.exp(own_piece - top)
    total = jnp.sum(probs, axis=-1) + own_probability
    mixed_values = jnp.einsum(
        "skgl,skld->skgd",
        probs.astype(jnp.bfloat16),
        value_cache_rows,
        preferred_element_type=jnp.float32,
    )
    fresh = fresh_value_heads.reshape(seqs_here, heads_kv, 1, HEAD_SIZE).astype(jnp.float32)
    mixed_values = (
        mixed_values + own_probability.astype(jnp.bfloat16).astype(jnp.float32)[..., None] * fresh
    )
    attended = (mixed_values / total[..., None]).astype(jnp.bfloat16).reshape(seqs_here, -1)
    slots = owners.shape[0]
    rows_piece = sectioned_rows.shape[1]
    numbers = jnp.arange(slots, dtype=jnp.int32)
    matches = (owners[:, None] == numbers[None, :]).astype(jnp.int32)
    piece_of_slot = jnp.sum(numbers[:, None] * matches, axis=0)
    blocks = attended.reshape(seqs_here, slots, rows_piece)
    by_slot = jnp.take(blocks, piece_of_slot, axis=1)
    partial_sum = jnp.einsum(
        "snr,nrd->sd",
        by_slot,
        lax.all_gather(sectioned_rows, "batch", axis=0, tiled=True),
        preferred_element_type=jnp.float32,
    )
    stream = residual.astype(jnp.float32) + lax.psum_scatter(
        partial_sum.astype(jnp.bfloat16), "tensor", scatter_dimension=1, tiled=True
    ).astype(jnp.float32)
    squares = lax.psum(jnp.sum(stream * stream, axis=1), "tensor")
    inverse_rms = lax.rsqrt(squares / D + 1e-06)
    normed = (stream * inverse_rms[:, None] * norm_gain.astype(jnp.float32)[None, :]).astype(
        jnp.bfloat16
    )
    return (stream.astype(jnp.bfloat16), normed)


def solution(mesh):
    return jax.shard_map(
        local,
        mesh=mesh,
        in_specs=(
            P("batch", "tensor"),
            P("batch", "tensor"),
            P("batch", "tensor"),
            P("batch", "tensor", None, None),
            P("batch", "tensor", None, None),
            P("batch"),
            P("batch", "tensor"),
            P("batch", "tensor", None),
            P(),
            P("tensor"),
        ),
        out_specs=(P("batch", "tensor"), P("batch", "tensor")),
        check_vma=False,
    )
```

profile of v0, /device:TPU:1, one launch (start us, length us, event | category | flops | bytes accessed | tf_op | source)
XLA Modules:
  0.0 198.9 jit_solution(1545661065794477938)
XLA Ops:
  7.2 0.0 copy-start
  7.2 0.0 all-gather.2.cloned.1.call-start
  7.2 0.7 all-gather.2.cloned.1.call-update
  7.9 0.0 reduce-scatter.4.cloned.1.call-start
  8.0 0.0 copy-start.1
  8.0 0.8 convert_element_type.43
  8.8 0.0 copy-done
  8.8 1.0 fusion.22
  9.8 0.7 iota_compare_fusion
  10.6 0.0 copy-start.4
  10.6 3.5 %fusion.32 = (f32[4,8]{1,0:T(4,128)S(1)}, f32[4,8,4096]{2,1,0:T(8,128)S(1)}) fusion(bf16[4,1,4096,128]{3,2,1,0:T(8,128)(2,1)} %param.13, bf16[1,4,8,128]{3,1,2,0:T(4,128)(2,1)} %bitcast.43, pred[4,4096]{1,0:T(4,128)(4,1)S(1)} %iota_compare_fusion), kind=kOutput, calls=%fused_computation.43 | convolution fusion | flops 33947616 | bytes 4743296 | tf_op jit(solution)/shard_map/skgd,skld->skgl/dot_general | solution.py:31
  14.1 0.3 fusion.14
  14.3 0.0 copy-done.1
  14.3 0.7 fusion.11
  15.0 0.1 reshape_reshape.3
  15.2 0.0 copy-done.4
  15.2 0.1 select_reduce_fusion
  15.3 0.6 gather_fusion
  15.9 0.0 copy-start.2
  15.9 0.0 copy-start.3
  15.9 72.9 %all-gather.2.cloned.1.call-done = bf16[32,32,5120]{2,1,0:T(8,128)(2,1)} async-done(((bf16[1,32,5120]{2,1,0:T(8,128)(2,1)}), bf16[32,32,5120]{2,1,0:T(8,128)(2,1)}) %all-gather.2.cloned.1.call-update) | async-done | bytes 10485776 | tf_op jit(solution)/shard_map/all_gather | solution.py:70
  88.9 5.0 %fusion = bf16[4,5120]{1,0:T(4,128)(2,1)S(1)} fusion(bf16[32,32,5120]{2,1,0:T(8,128)(2,1)} %all-gather.2.cloned.1.call-done, bf16[32,4,32]{2,1,0:T(4,128)(2,1)S(1)} %gather_fusion, pred[32]{0:T(512)(128)(4,1)S(1)} %compare_and_fusion), kind=kOutput, calls=%fused_computation.2 | convolution fusion | flops 41967616 | bytes 10534944 | tf_op jit(solution)/shard_map/snr,nrd->sd/dot_general | solution.py:67
  93.9 1.6 copy.17
  95.4 0.0 reduce-scatter.4.cloned.1.call-update
  95.5 76.4 %reduce-scatter.4.cloned.1.call-done = bf16[640,4]{1,0:T(8,128)(2,1)} async-done(((bf16[5120,4]{1,0:T(8,128)(2,1)}), bf16[640,4]{1,0:T(8,128)(2,1)}) %reduce-scatter.4.cloned.1.call-update) | async-done | bytes 5136
  171.9 1.0 copy.18
  172.9 0.0 copy-done.2
  172.9 0.1 multiply_reduce_fusion
  173.1 0.0 copy-done.3
  173.1 18.3 %psum.7 = f32[4]{0:T(128)S(1)} all-reduce(f32[4]{0:T(128)S(1)} %multiply_reduce_fusion), channel_id=1, replica_groups=mesh['batch'=32,'tensor'=8] {'tensor'}, use_global_device_ids=true, to_apply=%region_5.6 | all-reduce | flops 4 | bytes 32 | tf_op jit(solution)/shard_map/psum | solution.py:76
  191.4 0.7 multiply_convert_fusion
  (8 shorter events, 0.1 us)
Async XLA Ops:
  7.2 1.6 copy-start
  7.2 81.7 %all-gather.2.cloned.1.call-start = ((), (), s32[]{:S(2)}) async-start(), calls=%async_computation.1 | async-start | bytes 10813440 | tf_op jit(solution)/shard_map/all_gather | solution.py:70
  7.9 164.0 %reduce-scatter.4.cloned.1.call-start = ((), (), s32[]{:S(2)}) async-start(), calls=%async_computation.2 | async-start | bytes 1474560
  8.0 6.4 %copy-start.1 = (bf16[4,1,4096,128]{3,2,1,0:T(8,128)(2,1)S(1)}, bf16[4,1,4096,128]{3,2,1,0:T(8,128)(2,1)}, u32[]{:S(2)}) copy-start(bf16[4,1,4096,128]{3,2,1,0:T(8,128)(2,1)} %param.14) | copy-start | bytes 12582916
  10.6 4.6 %copy-start.4 = (s32[32]{0:T(128)S(1)}, s32[32]{0:T(128)}, u32[]{:S(2)}) copy-start(s32[32]{0:T(128)} %param.18) | copy-start | bytes 388
  15.9 157.0 %copy-start.2 = (bf16[4,640]{1,0:T(4,128)(2,1)S(1)}, bf16[4,640]{1,0:T(4,128)(2,1)}, u32[]{:S(2)}) copy-start(bf16[4,640]{1,0:T(4,128)(2,1)} %param.16) | copy-start | bytes 15364
  15.9 157.1 %copy-start.3 = (bf16[640]{0:T(1024)(128)(2,1)S(1)}, bf16[640]{0:T(1024)(128)(2,1)}, u32[]{:S(2)}) copy-start(bf16[640]{0:T(1024)(128)(2,1)} %param.19) | copy-start | bytes 3844
Sparse Core Ops, SparseCore 0:
  9.9 78.9 all-gather.1
  95.6 76.2 reduce-scatter.3
where the time goes:
time: 203 us; the launch traced here: 199 us
  waiting for transfers between devices  150 us (74%)
  blocking collectives  18.3 us (9%)
  between operations  14.1 us (7%)
  matrix products  10.2 us (5%)
  local copies, waits for them, and re-layouts  3.33 us (2%)
  other arithmetic  2.78 us (1%)
    unnamed x3, waiting for transfers between devices  77.1 us
    all_gather x1, waiting for transfers between devices, local(): lax.all_gather(sectioned_rows, 'batch', axis=0, tiled=True)  72.9 us
    psum x1, blocking collectives, local(): squares = lax.psum(jnp.sum(stream * stream, axis=1), 'tensor')  18.3 us
    dot_general x1, matrix products, local(): jnp.einsum('snr,nrd->sd', by_slot, lax.all_gather(sectioned_rows, 'batch'...  4.99 us
  transfers between devices with their start and end apart: 2, of which 2 were waited for; matrix products, arithmetic and copies ran while one was open for 4% of the time, Pallas kernels for 0%

commit v1 on v0

v1 whole, which is shorter than its diff:
```python
import functools

import jax
import jax.numpy as jnp
from jax import lax
from jax.experimental import pallas as pl
from jax.experimental.pallas import tpu as pltpu
from jax.sharding import PartitionSpec as P

D = 5120
HEAD_SIZE = 128
HEADS = 8
SEQS = 4
SPAN = 4096
BATCH = 32
TENSOR = 8
GROUP = 8
CLANS = BATCH // GROUP
PIECE = 32
SLICE = D // TENSOR
FOLD = 384
REST = SLICE - FOLD
MESH = pl.DeviceIdType.MESH


def place_of(batch):
    y_lo, z, core = batch // 16, (batch // 2) % 8, batch % 2
    return (z // 2) * 8 + y_lo * 4 + (z % 2) * 2 + core


def batch_of(place):
    clan, y_lo, z_lo, core = place // 8, (place // 4) % 2, (place // 2) % 2, place % 2
    return y_lo * 16 + (clan * 2 + z_lo) * 2 + core


def slice_of(member, tensor):
    y_lo, z_lo, core = member // 4, (member // 2) % 2, member % 2
    x, y_hi = tensor // 2, tensor % 2
    return ((x + 2 * core + (y_lo + z_lo) % 2) % 4) * 2 + (y_hi + z_lo) % 2


def member_of(part, tensor):
    x, y_hi = tensor // 2, tensor % 2
    step = (part // 2 - x + 4) % 4
    z_lo = (part % 2 - y_hi + 2) % 2
    y_lo = (step % 2 + z_lo) % 2
    return y_lo * 4 + z_lo * 2 + step // 2


def kernel(
    q_ref,
    fresh_k_ref,
    fresh_v_ref,
    keys_hbm,
    values_hbm,
    lengths_ref,
    residual_ref,
    rows_hbm,
    owners_ref,
    gain_ref,
    stream_ref,
    normed_ref,
    keys,
    values,
    q_by_head,
    weights,
    attended,
    message,
    gathered,
    rows,
    partial,
    partials,
    square,
    squares,
    key_sem,
    value_sem,
    rows_send,
    rows_recv,
    att_send,
    att_recv,
    part_send,
    part_recv,
    sq_send,
    sq_recv,
):
    batch, tensor = lax.axis_index("batch"), lax.axis_index("tensor")
    place = place_of(batch)
    clan, member = place // GROUP, place % GROUP
    part = slice_of(member, tensor)
    mine = part == tensor

    for s in range(SEQS):
        pltpu.make_async_copy(keys_hbm.at[s, 0], keys.at[s], key_sem.at[s]).start()
    for s in range(SEQS):
        pltpu.make_async_copy(values_hbm.at[s, 0], values.at[s], value_sem.at[s]).start()

    barrier = pltpu.get_barrier_semaphore()

    def greet_batch(step, carry):
        pl.semaphore_signal(
            barrier, inc=1, device_id=((batch + step) % BATCH, tensor), device_id_type=MESH
        )
        return carry

    def greet_tensor(step, carry):
        pl.semaphore_signal(
            barrier, inc=1, device_id=(batch, (tensor + step) % TENSOR), device_id_type=MESH
        )
        return carry

    def greet_sources(step, carry):
        source = (tensor * CLANS + clan + step) % BATCH
        t = source // CLANS
        b = batch_of((source % CLANS) * GROUP + member_of(tensor, t))

        @pl.when(jnp.logical_not((b == batch) & (t == tensor)))
        def _():
            pl.semaphore_signal(barrier, inc=1, device_id=(b, t), device_id_type=MESH)

        return carry

    lax.fori_loop(1, BATCH, greet_batch, 0)
    lax.fori_loop(1, TENSOR, greet_tensor, 0)
    lax.fori_loop(0, BATCH, greet_sources, 0)
    pl.semaphore_wait(barrier, BATCH - 1 + TENSOR - 1 + BATCH - jnp.where(mine, 1, 0))

    def send_rows(step, carry):
        other = (member + step) % GROUP
        pltpu.make_async_remote_copy(
            src_ref=rows_hbm.at[0, :, pl.ds(pl.multiple_of(slice_of(other, tensor) * SLICE, 128), SLICE)],
            dst_ref=rows.at[member],
            send_sem=rows_send,
            recv_sem=rows_recv,
            device_id=(batch_of(clan * GROUP + other), tensor),
            device_id_type=MESH,
        ).start()
        return carry

    lax.fori_loop(1, GROUP, send_rows, 0)
    pltpu.make_async_copy(
        rows_hbm.at[0, :, pl.ds(pl.multiple_of(part * SLICE, 128), SLICE)],
        rows.at[member],
        rows_recv,
    ).start()

    q_all = q_ref[...].astype(jnp.float32)
    for h in range(HEADS):
        q_by_head[pl.ds(h, SEQS, stride=HEADS), :] = q_all[:, h * HEAD_SIZE : (h + 1) * HEAD_SIZE]
    fresh_k = fresh_k_ref[...].astype(jnp.float32)
    fresh_v = fresh_v_ref[...].astype(jnp.float32)
    scale = HEAD_SIZE ** (-0.5)
    position = lax.broadcasted_iota(jnp.int32, (HEADS, SPAN), 1)
    own_weights, totals = [], []
    for s in range(SEQS):
        pltpu.make_async_copy(keys_hbm.at[s, 0], keys.at[s], key_sem.at[s]).wait()
        q = q_by_head[s * HEADS : (s + 1) * HEADS, :]
        scores = (
            lax.dot_general(
                q.astype(jnp.bfloat16),
                keys[s],
                (((1,), (1,)), ((), ())),
                preferred_element_type=jnp.float32,
            )
            * scale
        )
        scores = jnp.where(position < lengths_ref[s], scores, -1e30)
        own = jnp.sum(q * fresh_k[s : s + 1, :], axis=1, keepdims=True) * scale
        top = jnp.maximum(jnp.max(scores, axis=1, keepdims=True), own)
        prob = jnp.exp(scores - top)
        own_prob = jnp.exp(own - top)
        totals.append(jnp.sum(prob, axis=1, keepdims=True) + own_prob)
        own_weights.append(own_prob.astype(jnp.bfloat16).astype(jnp.float32))
        weights[s] = prob.astype(jnp.bfloat16)
    for s in range(SEQS):
        pltpu.make_async_copy(values_hbm.at[s, 0], values.at[s], value_sem.at[s]).wait()
        mixed = lax.dot_general(
            weights[s], values[s], (((1,), (0,)), ((), ())), preferred_element_type=jnp.float32
        )
        mixed = (mixed + own_weights[s] * fresh_v[s : s + 1, :]) / totals[s]
        attended[s * HEADS : (s + 1) * HEADS, :] = mixed
        attended[(s + SEQS) * HEADS : (s + SEQS + 1) * HEADS, :] = mixed

    row = lax.broadcasted_iota(jnp.int32, (8, 128), 0)
    lane = lax.broadcasted_iota(jnp.int32, (8, 128), 1)
    code = (row // SEQS) * 4 + lane // PIECE
    blocks = [jnp.zeros((8, 128), jnp.float32)] * CLANS
    for k in range(BATCH):
        if k % 4 == 0:
            head = attended[pl.ds(k // 4, 8, stride=HEADS), :]
        target = place_of(owners_ref[k])
        turned = pltpu.roll(head, (target % 4 + 4 - k % 4) % 4 * PIECE, 1)
        blocks = [
            jnp.where(code == target - c * GROUP, turned, blocks[c]) for c in range(CLANS)
        ]
    for c in range(CLANS):
        message[c] = blocks[c].astype(jnp.bfloat16)

    def send_attended(step, carry):
        other = (place + step) % BATCH
        pltpu.make_async_remote_copy(
            src_ref=message.at[other // GROUP],
            dst_ref=gathered.at[batch],
            send_sem=att_send,
            recv_sem=att_recv,
            device_id=(batch_of(other), tensor),
            device_id_type=MESH,
        ).start()
        return carry

    lax.fori_loop(1, BATCH, send_attended, 0)
    pltpu.make_async_copy(message.at[clan], gathered.at[batch], att_recv).start()

    pad = jnp.zeros((SEQS, FOLD - REST), jnp.float32)

    def fold(x):
        return jnp.concatenate(
            [x[:, :FOLD], jnp.concatenate([x[:, FOLD:], pad], axis=1)], axis=0
        )

    residual = fold(residual_ref[...].astype(jnp.float32))
    gain = fold(jnp.broadcast_to(gain_ref[...].astype(jnp.float32), (SEQS, SLICE)))
    row3 = lax.broadcasted_iota(jnp.int32, (8, FOLD), 0)
    lane3 = lax.broadcasted_iota(jnp.int32, (8, FOLD), 1)
    used = (row3 < SEQS) | (lane3 < REST)

    pltpu.make_async_copy(rows, rows, rows_recv).wait()
    pltpu.make_async_copy(gathered, gathered, att_recv).wait()

    first = gathered[...].astype(jnp.float32)
    swapped = pltpu.roll(first, SEQS, 1).reshape(BATCH * 8, 128).astype(jnp.bfloat16)
    first = first.reshape(BATCH * 8, 128).astype(jnp.bfloat16)
    table = rows[...].reshape(GROUP * PIECE, SLICE)
    low = jnp.dot(
        jnp.concatenate([first, swapped], axis=1), table[:, :FOLD], preferred_element_type=jnp.float32
    )
    high = jnp.dot(
        jnp.concatenate([swapped, first], axis=1), table[:, FOLD:], preferred_element_type=jnp.float32
    )
    upper = lax.broadcasted_iota(jnp.int32, (BATCH * 8, REST), 0) % 8 < SEQS
    partial[:, :, :REST] = (
        jnp.where(upper, low[:, :REST], high).reshape(BATCH, 8, REST).astype(jnp.bfloat16)
    )
    partial[:, :, REST:] = low[:, REST:].reshape(BATCH, 8, FOLD - REST).astype(jnp.bfloat16)

    def send_partial(step, carry):
        other = (batch + step) % BATCH
        local = mine & (step == 0)

        @pl.when(jnp.logical_not(local))
        def _():
            pltpu.make_async_remote_copy(
                src_ref=partial.at[other],
                dst_ref=partials.at[tensor * CLANS + clan],
                send_sem=part_send,
                recv_sem=part_recv,
                device_id=(other, part),
                device_id_type=MESH,
            ).start()

        @pl.when(local)
        def _():
            pltpu.make_async_copy(
                partial.at[other], partials.at[tensor * CLANS + clan], part_recv
            ).start()

        return carry

    lax.fori_loop(0, BATCH, send_partial, 0)
    pltpu.make_async_copy(partials, partials, part_recv).wait()
    total = jnp.sum(partials[...].astype(jnp.float32), axis=0)
    stream = jnp.where(used, residual + total, 0.0)

    squared = stream * stream
    squared = squared[:, :128] + squared[:, 128:256] + squared[:, 256:]
    squared = squared + pltpu.roll(squared, SEQS, 0)
    square[...] = jnp.broadcast_to(jnp.sum(squared, axis=1, keepdims=True), (8, 128))

    def send_square(step, carry):
        pltpu.make_async_remote_copy(
            src_ref=square,
            dst_ref=squares.at[step - 1],
            send_sem=sq_send,
            recv_sem=sq_recv,
            device_id=(batch, (tensor + step) % TENSOR),
            device_id_type=MESH,
        ).start()
        return carry

    lax.fori_loop(1, TENSOR, send_square, 0)

    def unfold(x):
        return jnp.concatenate([x[:SEQS, :], x[SEQS:, :REST]], axis=1)

    stream_ref[...] = unfold(stream).astype(jnp.bfloat16)
    scaled = stream * gain
    pltpu.make_async_copy(squares, squares, sq_recv).wait()
    mean = (square[...] + jnp.sum(squares[...], axis=0)) / D
    inverse = lax.rsqrt(mean + 1e-6)[:, :1]
    normed_ref[...] = unfold(scaled * inverse).astype(jnp.bfloat16)

    pltpu.make_async_copy(squares, squares, sq_send).wait()
    pltpu.make_async_copy(rows.at[: GROUP - 1], rows.at[: GROUP - 1], rows_send).wait()
    pltpu.make_async_copy(gathered.at[: BATCH - 1], gathered.at[: BATCH - 1], att_send).wait()
    pltpu.make_async_copy(partial.at[: BATCH - 1], partial.at[: BATCH - 1], part_send).wait()

    @pl.when(jnp.logical_not(mine))
    def _():
        pltpu.make_async_copy(partial.at[0], partial.at[0], part_send).wait()


def local(
    queries,
    fresh_key_heads,
    fresh_value_heads,
    cached_keys,
    value_cache_rows,
    lengths,
    residual,
    sectioned_rows,
    owners,
    norm_gain,
):
    vmem = pl.BlockSpec(memory_space=pltpu.VMEM)
    smem = pl.BlockSpec(memory_space=pltpu.SMEM)
    anywhere = pl.BlockSpec(memory_space=pl.ANY)
    block = jax.ShapeDtypeStruct((SEQS, SLICE), jnp.bfloat16)
    bf16, f32 = jnp.bfloat16, jnp.float32
    return pl.pallas_call(
        kernel,
        out_shape=(block, block),
        in_specs=[vmem, vmem, vmem, anywhere, anywhere, smem, vmem, anywhere, smem, vmem],
        out_specs=(vmem, vmem),
        scratch_shapes=[
            pltpu.VMEM((SEQS, SPAN, HEAD_SIZE), bf16),
            pltpu.VMEM((SEQS, SPAN, HEAD_SIZE), bf16),
            pltpu.VMEM((SEQS * HEADS, HEAD_SIZE), f32),
            pltpu.VMEM((SEQS, HEADS, SPAN), bf16),
            pltpu.VMEM((2 * SEQS * HEADS, HEAD_SIZE), f32),
            pltpu.VMEM((CLANS, 8, 128), bf16),
            pltpu.VMEM((BATCH, 8, 128), bf16),
            pltpu.VMEM((GROUP, PIECE, SLICE), bf16),
            pltpu.VMEM((BATCH, 8, FOLD), bf16),
            pltpu.VMEM((BATCH, 8, FOLD), bf16),
            pltpu.VMEM((8, 128), f32),
            pltpu.VMEM((TENSOR - 1, 8, 128), f32),
            pltpu.SemaphoreType.DMA((SEQS,)),
            pltpu.SemaphoreType.DMA((SEQS,)),
        ]
        + [pltpu.SemaphoreType.DMA] * 8,
        compiler_params=pltpu.CompilerParams(
            collective_id=0, has_side_effects=True, vmem_limit_bytes=56 * 1024 * 1024
        ),
    )(
        queries,
        fresh_key_heads,
        fresh_value_heads,
        cached_keys,
        value_cache_rows,
        lengths,
        residual,
        sectioned_rows,
        owners,
        norm_gain.reshape(1, -1),
    )


def solution(mesh):
    return jax.shard_map(
        local,
        mesh=mesh,
        in_specs=(
            P("batch", "tensor"),
            P("batch", "tensor"),
            P("batch", "tensor"),
            P("batch", "tensor", None, None),
            P("batch", "tensor", None, None),
            P("batch"),
            P("batch", "tensor"),
            P("batch", "tensor", None),
            P(),
            P("tensor"),
        ),
        out_specs=(P("batch", "tensor"), P("batch", "tensor")),
        check_vma=False,
    )
```

time: 203 us -> 43.2 us (0.21); the launches traced: 199 us -> 43 us
  waiting for transfers between devices: 150 us -> 0 us
  Pallas kernels: 0 us -> 38.5 us
  blocking collectives: 18.3 us -> 0 us
  between operations: 14.1 us -> 0.64 us
  matrix products: 10.2 us -> 0 us
  other arithmetic: 2.78 us -> 0 us
    unnamed x3 -> x0, waiting for transfers between devices: 77.1 us -> none
    all_gather x1 -> x0, waiting for transfers between devices: 72.9 us -> none  [local(): lax.all_gather(sectioned_rows, 'batch', axis=0, tiled=True)]
    pallas_call x0 -> x1, Pallas kernels: none -> 38.5 us  [local(): pl.pallas_call(kernel, out_shape=(block, block), in_specs=[vmem, vmem, vm...]
    psum x1 -> x0, blocking collectives: 18.3 us -> none  [local(): squares = lax.psum(jnp.sum(stream * stream, axis=1), 'tensor')]
    dot_general x4 -> x0, matrix products: 10.2 us -> none  [the longest x1 4.99 us: local(): jnp.einsum('snr,nrd->sd', by_slot, lax.all_gather(sectioned_rows, 'batch'...]
  transfers between devices with their start and end apart: 2 -> 0, of which waited for: 2 -> 0; matrix products, arithmetic and copies ran while one was open for 4% -> 0% of each run, Pallas kernels for 0% -> 0%
where the time goes in v1:
time: 43.2 us; the launch traced here: 43 us
  Pallas kernels  38.5 us (89%)
  local copies, waits for them, and re-layouts  3.84 us (9%)
  between operations  0.64 us (1%)
    pallas_call x1, Pallas kernels, local(): pl.pallas_call(kernel, out_shape=(block, block), in_specs=[vmem, vmem, vm...  38.5 us
    unnamed x2, local copies, waits for them, and re-layouts  2.57 us
    reshape x1, local copies, waits for them, and re-layouts, local(): norm_gain.reshape(1, -1)  1.26 us

profile of v1, /device:TPU:1, one launch (start us, length us, event | category | flops | bytes accessed | tf_op | source)
XLA Modules:
  0.0 43.0 jit_solution(6294760776282106756)
XLA Ops:
  0.6 1.3 %reshape.7.gain_ref = bf16[1,640]{1,0:T(2,128)(2,1)} reshape(bf16[640]{0:T(1024)(128)(2,1)} %param.19) | data formatting | bytes 2560 | tf_op jit(solution)/shard_map/reshape | solution.py:363
  1.9 38.5 %shard_map.113 = (bf16[4,640]{1,0:T(4,128)(2,1)}, bf16[4,640]{1,0:T(4,128)(2,1)}) custom-call(bf16[4,1024]{1,0:T(4,128)(2,1)} %q_ref.1, bf16[4,128]{1,0:T(4,128)(2,1)} %fresh_k_ref.1, bf16[4,128]{1,0:T(4,128)(2,1)} %fresh_v_ref.1, bf16[4,1,4096,128]{3,2,1,0:T(8,128)(2,1)} %keys_hbm.1, bf16[4,1,4096,128]{3,2,1,0:T(8,128)(2,1)} %values_hbm.1, s32[4]{0:T(128)} %lengths_ref.1, ...), custom_call_target="tpu_custom_call" | custom-call | tf_op jit(solution)/shard_map/pallas_call | solution.py:328
  40.4 1.3 %copy.14 = bf16[4,640]{1,0:T(4,128)(2,1)} copy(bf16[4,640]{1,0:T(4,128)(2,1)} %get-tuple-element.4) | data formatting | bytes 10240
  41.7 1.3 %copy.15 = bf16[4,640]{1,0:T(4,128)(2,1)} copy(bf16[4,640]{1,0:T(4,128)(2,1)} %get-tuple-element.5) | data formatting | bytes 10240

commit v2 on v1

--- a/solution.py
+++ b/solution.py
@@ -47,19 +47,39 @@
     return y_lo * 4 + z_lo * 2 + step // 2
 
 
+def batch_at(batch, step):
+    y_lo, z, core = batch // 16, (batch // 2) % 8, batch % 2
+    ring, rest = step // 4, step % 4
+    away = 4 + (ring // 2 + ring % 2) * (1 - 2 * (ring % 2))
+    return (
+        (y_lo + 1 - rest // 2) % 2 * 16 + (z + away) % 8 * 2 + (core + 1 - rest % 2) % 2
+    )
+
+
+def tensor_at(tensor, step):
+    x, y_hi = tensor // 2, tensor % 2
+    ring = step // 2
+    away = 2 + (ring // 2 + ring % 2) * (1 - 2 * (ring % 2))
+    return (x + away) % 4 * 2 + (y_hi + 1 - step % 2) % 2
+
+
 def kernel(
+    q_hbm,
+    fresh_k_hbm,
+    fresh_v_hbm,
+    keys_hbm,
+    values_hbm,
+    lengths_hbm,
+    residual_hbm,
+    rows_hbm,
+    owners_hbm,
+    out_ref,
     q_ref,
     fresh_k_ref,
     fresh_v_ref,
-    keys_hbm,
-    values_hbm,
     lengths_ref,
     residual_ref,
-    rows_hbm,
     owners_ref,
-    gain_ref,
-    stream_ref,
-    normed_ref,
     keys,
     values,
     q_by_head,
@@ -72,6 +92,7 @@
     partials,
     square,
     squares,
+    small_sem,
     key_sem,
     value_sem,
     rows_send,
@@ -89,40 +110,44 @@
     part = slice_of(member, tensor)
     mine = part == tensor
 
+    barrier = pltpu.get_barrier_semaphore()
+
+    def greet_batch(step, carry):
+        pl.semaphore_signal(
+            barrier, inc=1, device_id=(batch_at(batch, step), tensor), device_id_type=MESH
+        )
+        return carry
+
+    def greet_tensor(step, carry):
+        pl.semaphore_signal(
+            barrier, inc=1, device_id=(batch, tensor_at(tensor, step)), device_id_type=MESH
+        )
+        return carry
+
+    lax.fori_loop(0, BATCH - 1, greet_batch, 0)
+    lax.fori_loop(0, TENSOR - 1, greet_tensor, 0)
+
+    small = [
+        pltpu.make_async_copy(source, target, small_sem.at[i])
+        for i, (source, target) in enumerate(
+            (
+                (q_hbm, q_ref),
+                (fresh_k_hbm, fresh_k_ref),
+                (fresh_v_hbm, fresh_v_ref),
+                (lengths_hbm, lengths_ref),
+                (residual_hbm, residual_ref),
+                (owners_hbm, owners_ref),
+            )
+        )
+    ]
+    for copy in small:
+        copy.start()
     for s in range(SEQS):
         pltpu.make_async_copy(keys_hbm.at[s, 0], keys.at[s], key_sem.at[s]).start()
     for s in range(SEQS):
         pltpu.make_async_copy(values_hbm.at[s, 0], values.at[s], value_sem.at[s]).start()
 
-    barrier = pltpu.get_barrier_semaphore()
-
-    def greet_batch(step, carry):
-        pl.semaphore_signal(
-            barrier, inc=1, device_id=((batch + step) % BATCH, tensor), device_id_type=MESH
-        )
-        return carry
-
-    def greet_tensor(step, carry):
-        pl.semaphore_signal(
-            barrier, inc=1, device_id=(batch, (tensor + step) % TENSOR), device_id_type=MESH
-        )
-        return carry
-
-    def greet_sources(step, carry):
-        source = (tensor * CLANS + clan + step) % BATCH
-        t = source // CLANS
-        b = batch_of((source % CLANS) * GROUP + member_of(tensor, t))
-
-        @pl.when(jnp.logical_not((b == batch) & (t == tensor)))
-        def _():
-            pl.semaphore_signal(barrier, inc=1, device_id=(b, t), device_id_type=MESH)
-
-        return carry
-
-    lax.fori_loop(1, BATCH, greet_batch, 0)
-    lax.fori_loop(1, TENSOR, greet_tensor, 0)
-    lax.fori_loop(0, BATCH, greet_sources, 0)
-    pl.semaphore_wait(barrier, BATCH - 1 + TENSOR - 1 + BATCH - jnp.where(mine, 1, 0))
+    pl.semaphore_wait(barrier, BATCH - 1 + TENSOR - 1)
 
     def send_rows(step, carry):
         other = (member + step) % GROUP
@@ -143,6 +168,8 @@
         rows_recv,
     ).start()
 
+    for copy in small:
+        copy.wait()
     q_all = q_ref[...].astype(jnp.float32)
     for h in range(HEADS):
         q_by_head[pl.ds(h, SEQS, stride=HEADS), :] = q_all[:, h * HEAD_SIZE : (h + 1) * HEAD_SIZE]
@@ -196,18 +223,18 @@
         message[c] = blocks[c].astype(jnp.bfloat16)
 
     def send_attended(step, carry):
-        other = (place + step) % BATCH
+        other = batch_at(batch, step)
         pltpu.make_async_remote_copy(
-            src_ref=message.at[other // GROUP],
+            src_ref=message.at[place_of(other) // GROUP],
             dst_ref=gathered.at[batch],
             send_sem=att_send,
             recv_sem=att_recv,
-            device_id=(batch_of(other), tensor),
+            device_id=(other, tensor),
             device_id_type=MESH,
         ).start()
         return carry
 
-    lax.fori_loop(1, BATCH, send_attended, 0)
+    lax.fori_loop(0, BATCH - 1, send_attended, 0)
     pltpu.make_async_copy(message.at[clan], gathered.at[batch], att_recv).start()
 
     pad = jnp.zeros((SEQS, FOLD - REST), jnp.float32)
@@ -218,7 +245,6 @@
         )
 
     residual = fold(residual_ref[...].astype(jnp.float32))
-    gain = fold(jnp.broadcast_to(gain_ref[...].astype(jnp.float32), (SEQS, SLICE)))
     row3 = lax.broadcasted_iota(jnp.int32, (8, FOLD), 0)
     lane3 = lax.broadcasted_iota(jnp.int32, (8, FOLD), 1)
     used = (row3 < SEQS) | (lane3 < REST)
@@ -243,8 +269,8 @@
     partial[:, :, REST:] = low[:, REST:].reshape(BATCH, 8, FOLD - REST).astype(jnp.bfloat16)
 
     def send_partial(step, carry):
-        other = (batch + step) % BATCH
-        local = mine & (step == 0)
+        other = batch_at(batch, step)
+        local = mine & (step == BATCH - 1)
 
         @pl.when(jnp.logical_not(local))
         def _():
@@ -278,25 +304,24 @@
     def send_square(step, carry):
         pltpu.make_async_remote_copy(
             src_ref=square,
-            dst_ref=squares.at[step - 1],
+            dst_ref=squares.at[step],
             send_sem=sq_send,
             recv_sem=sq_recv,
-            device_id=(batch, (tensor + step) % TENSOR),
+            device_id=(batch, tensor_at(tensor, step)),
             device_id_type=MESH,
         ).start()
         return carry
 
-    lax.fori_loop(1, TENSOR, send_square, 0)
+    lax.fori_loop(0, TENSOR - 1, send_square, 0)
 
     def unfold(x):
         return jnp.concatenate([x[:SEQS, :], x[SEQS:, :REST]], axis=1)
 
-    stream_ref[...] = unfold(stream).astype(jnp.bfloat16)
-    scaled = stream * gain
+    out_ref[0] = unfold(stream)
     pltpu.make_async_copy(squares, squares, sq_recv).wait()
     mean = (square[...] + jnp.sum(squares[...], axis=0)) / D
     inverse = lax.rsqrt(mean + 1e-6)[:, :1]
-    normed_ref[...] = unfold(scaled * inverse).astype(jnp.bfloat16)
+    out_ref[1] = unfold(stream * inverse)
 
     pltpu.make_async_copy(squares, squares, sq_send).wait()
     pltpu.make_async_copy(rows.at[: GROUP - 1], rows.at[: GROUP - 1], rows_send).wait()
@@ -320,17 +345,20 @@
     owners,
     norm_gain,
 ):
-    vmem = pl.BlockSpec(memory_space=pltpu.VMEM)
-    smem = pl.BlockSpec(memory_space=pltpu.SMEM)
     anywhere = pl.BlockSpec(memory_space=pl.ANY)
-    block = jax.ShapeDtypeStruct((SEQS, SLICE), jnp.bfloat16)
     bf16, f32 = jnp.bfloat16, jnp.float32
-    return pl.pallas_call(
+    out = pl.pallas_call(
         kernel,
-        out_shape=(block, block),
-        in_specs=[vmem, vmem, vmem, anywhere, anywhere, smem, vmem, anywhere, smem, vmem],
-        out_specs=(vmem, vmem),
+        out_shape=jax.ShapeDtypeStruct((2, SEQS, SLICE), f32),
+        in_specs=[anywhere] * 9,
+        out_specs=pl.BlockSpec(memory_space=pltpu.VMEM),
         scratch_shapes=[
+            pltpu.VMEM((SEQS, HEADS * HEAD_SIZE), bf16),
+            pltpu.VMEM((SEQS, HEAD_SIZE), bf16),
+            pltpu.VMEM((SEQS, HEAD_SIZE), bf16),
+            pltpu.SMEM((SEQS,), jnp.int32),
+            pltpu.VMEM((SEQS, SLICE), bf16),
+            pltpu.SMEM((BATCH,), jnp.int32),
             pltpu.VMEM((SEQS, SPAN, HEAD_SIZE), bf16),
             pltpu.VMEM((SEQS, SPAN, HEAD_SIZE), bf16),
             pltpu.VMEM((SEQS * HEADS, HEAD_SIZE), f32),
@@ -343,6 +371,7 @@
             pltpu.VMEM((BATCH, 8, FOLD), bf16),
             pltpu.VMEM((8, 128), f32),
             pltpu.VMEM((TENSOR - 1, 8, 128), f32),
+            pltpu.SemaphoreType.DMA((6,)),
             pltpu.SemaphoreType.DMA((SEQS,)),
             pltpu.SemaphoreType.DMA((SEQS,)),
         ]
@@ -360,8 +389,8 @@
         residual,
         sectioned_rows,
         owners,
-        norm_gain.reshape(1, -1),
-    )
+    )
+    return out[0].astype(bf16), (out[1] * norm_gain.astype(f32)).astype(bf16)
 
 
 def solution(mesh):

time: 43.2 us -> 37.5 us (0.87)
  Pallas kernels: 38.5 us -> 33.4 us
  local copies, waits for them, and re-layouts: 3.84 us -> 1.3 us
  other arithmetic: 0 us -> 1.99 us
    pallas_call x1, Pallas kernels: 38.5 us -> 33.4 us  [local(): pl.pallas_call(kernel, out_shape=jax.ShapeDtypeStruct((2, SEQS, SLICE), f...]
    unnamed x2 -> x0, local copies, waits for them, and re-layouts: 2.57 us -> none
    convert_element_type x0 -> x2, other arithmetic: none -> 1.99 us  [local(): return (out[0].astype(bf16), (out[1] * norm_gain.astype(f32)).astype(bf16))]
    convert_element_type x0 -> x1, local copies, waits for them, and re-layouts: none -> 1.3 us  [local(): return (out[0].astype(bf16), (out[1] * norm_gain.astype(f32)).astype(bf16))]
    reshape x1 -> x0, local copies, waits for them, and re-layouts: 1.26 us -> none  [local(): norm_gain.reshape(1, -1)]
where the time goes in v2:
time: 37.5 us; the launch traced here: 37.3 us
  Pallas kernels  33.4 us (89%)
  other arithmetic  1.99 us (5%)
  local copies, waits for them, and re-layouts  1.3 us (3%)
  between operations  0.64 us (2%)
    pallas_call x1, Pallas kernels, local(): pl.pallas_call(kernel, out_shape=jax.ShapeDtypeStruct((2, SEQS, SLICE), f...  33.4 us
    convert_element_type x2, other arithmetic, local(): return (out[0].astype(bf16), (out[1] * norm_gain.astype(f32)).astype(bf16))  1.99 us
    convert_element_type x1, local copies, waits for them, and re-layouts, local(): return (out[0].astype(bf16), (out[1] * norm_gain.astype(f32)).astype(bf16))  1.3 us

profile of v2, /device:TPU:1, one launch (start us, length us, event | category | flops | bytes accessed | tf_op | source)
XLA Modules:
  0.0 37.3 jit_solution(7723118703192557229)
XLA Ops:
  0.6 0.7 %convert_element_type.11 = f32[640]{0:T(1024)S(1)} convert(bf16[640]{0:T(1024)(128)(2,1)} %param.19) | non-fusion elementwise | flops 640 | bytes 3840 | tf_op jit(solution)/shard_map/convert_element_type | solution.py:393
  1.3 33.4 %shard_map.113 = f32[2,4,640]{2,1,0:T(4,128)} custom-call(bf16[4,1024]{1,0:T(4,128)(2,1)} %q_hbm.1, bf16[4,128]{1,0:T(4,128)(2,1)} %fresh_k_hbm.1, bf16[4,128]{1,0:T(4,128)(2,1)} %fresh_v_hbm.1, bf16[4,1,4096,128]{3,2,1,0:T(8,128)(2,1)} %keys_hbm.1, bf16[4,1,4096,128]{3,2,1,0:T(8,128)(2,1)} %values_hbm.1, s32[4]{0:T(128)} %lengths_hbm.1, ...), custom_call_target="tpu_custom_call" | custom-call | tf_op jit(solution)/shard_map/pallas_call | solution.py:350
  34.7 1.3 %fusion = bf16[4,640]{1,0:T(4,128)(2,1)} fusion(f32[2,4,640]{2,1,0:T(4,128)} %shard_map.113, f32[640]{0:T(1024)S(1)} %convert_element_type.11), kind=kLoop, calls=%fused_computation.2 | loop fusion | flops 5120 | bytes 17920 | tf_op jit(solution)/shard_map/convert_element_type | solution.py:393
  36.0 1.3 %fusion.1 = bf16[4,640]{1,0:T(4,128)(2,1)} fusion(f32[2,4,640]{2,1,0:T(4,128)} %shard_map.113), kind=kLoop, calls=%fused_computation.3 | loop fusion | bytes 10240 | tf_op jit(solution)/shard_map/convert_element_type | solution.py:393

commit v3 on v2

v3 whole, which is shorter than its diff:
```python
import functools

import jax
import jax.numpy as jnp
from jax import lax
from jax.experimental import pallas as pl
from jax.experimental.pallas import tpu as pltpu
from jax.sharding import PartitionSpec as P

D = 5120
HEAD_SIZE = 128
HEADS = 8
SEQS = 4
SPAN = 4096
BATCH = 32
TENSOR = 8
GROUP = 8
CLANS = BATCH // GROUP
PIECE = 32
SLICE = D // TENSOR
MESH = pl.DeviceIdType.MESH


def place_of(batch):
    return ((batch >> 2 & 3) << 3) + ((batch >> 4) << 2) + (batch & 3)


def batch_of(place):
    return ((place >> 2 & 1) << 4) + ((place >> 3) << 2) + (place & 3)


def slice_of(member, tensor):
    step = 2 * (member & 1) + ((member >> 2) ^ (member >> 1 & 1))
    return ((tensor + 2 * step) & 7) ^ (member >> 1 & 1)


def batch_at(batch, step):
    ring, rest = step >> 2, 3 - (step & 3)
    away = 4 + ((ring + 1) >> 1) * (1 - 2 * (ring & 1))
    return ((batch & 16) ^ ((rest & 2) << 3)) + ((((batch & 15) + 2 * away) & 15) ^ (rest & 1))


def tensor_at(tensor, step):
    ring = step >> 1
    away = 2 + ((ring + 1) >> 1) * (1 - 2 * (ring & 1))
    return ((tensor + 2 * away) & 7) ^ (1 - (step & 1))


def kernel(
    q_hbm,
    fresh_k_hbm,
    fresh_v_hbm,
    keys_hbm,
    values_hbm,
    lengths_hbm,
    residual_hbm,
    rows_hbm,
    owners_hbm,
    out_ref,
    q_ref,
    fresh_k_ref,
    fresh_v_ref,
    lengths_ref,
    residual_ref,
    owners_ref,
    keys,
    values,
    q_by_head,
    weights,
    attended,
    goals,
    message,
    gathered,
    rows,
    partial,
    partials,
    square,
    squares,
    small_sem,
    key_sem,
    value_sem,
    rows_send,
    rows_recv,
    att_send,
    att_recv,
    part_send,
    part_recv,
    sq_send,
    sq_recv,
):
    batch, tensor = lax.axis_index("batch"), lax.axis_index("tensor")
    place = place_of(batch)
    clan, member = place >> 3, place & 7
    part = slice_of(member, tensor)
    mine = part == tensor

    small = [
        pltpu.make_async_copy(source, target, small_sem.at[i])
        for i, (source, target) in enumerate(
            (
                (q_hbm, q_ref),
                (fresh_k_hbm, fresh_k_ref),
                (fresh_v_hbm, fresh_v_ref),
                (lengths_hbm, lengths_ref),
                (residual_hbm, residual_ref),
                (owners_hbm, owners_ref),
            )
        )
    ]
    for copy in small:
        copy.start()
    for s in range(SEQS):
        pltpu.make_async_copy(keys_hbm.at[s, 0], keys.at[s], key_sem.at[s]).start()
    for s in range(SEQS):
        pltpu.make_async_copy(values_hbm.at[s, 0], values.at[s], value_sem.at[s]).start()


    barrier = pltpu.get_barrier_semaphore()

    def greet_batch(step, carry):
        pl.semaphore_signal(
            barrier, inc=1, device_id=(batch_at(batch, step), tensor), device_id_type=MESH
        )
        return carry

    def greet_tensor(step, carry):
        pl.semaphore_signal(
            barrier, inc=1, device_id=(batch, tensor_at(tensor, step)), device_id_type=MESH
        )
        return carry

    lax.fori_loop(0, 4, greet_batch, 0)
    lax.fori_loop(0, TENSOR - 1, greet_tensor, 0)
    lax.fori_loop(4, BATCH - 1, greet_batch, 0)

    for copy in small:
        copy.wait()

    row = lax.broadcasted_iota(jnp.int32, (8, 128), 0)
    lane = lax.broadcasted_iota(jnp.int32, (8, 128), 1)
    block = lane // PIECE
    code = (row // SEQS) * 4 + block
    for h in range(HEADS):
        targets = [place_of(owners_ref[4 * h + j]) for j in range(4)]
        for r in range(4):
            goal = jnp.full((8, 128), targets[(3 - r) % 4], jnp.int32)
            for j in range(3):
                goal = jnp.where(block == j, targets[(j - r) % 4], goal)
            goals[h * 4 + r] = goal - code

    q_all = q_ref[...].astype(jnp.float32)
    for h in range(HEADS):
        q_by_head[pl.ds(h, SEQS, stride=HEADS), :] = q_all[:, h * HEAD_SIZE : (h + 1) * HEAD_SIZE]
    fresh_k = fresh_k_ref[...].astype(jnp.float32)
    fresh_v = fresh_v_ref[...].astype(jnp.float32)
    scale = HEAD_SIZE ** (-0.5)
    position = lax.broadcasted_iota(jnp.int32, (HEADS, SPAN), 1)
    for s in range(SEQS):
        pltpu.make_async_copy(keys_hbm.at[s, 0], keys.at[s], key_sem.at[s]).wait()
    own_weights, totals = [], []
    for s in range(SEQS):
        q = q_by_head[s * HEADS : (s + 1) * HEADS, :]
        scores = (
            lax.dot_general(
                q.astype(jnp.bfloat16),
                keys[s],
                (((1,), (1,)), ((), ())),
                preferred_element_type=jnp.float32,
            )
            * scale
        )
        scores = jnp.where(position < lengths_ref[s], scores, -1e30)
        own = jnp.sum(q * fresh_k[s : s + 1, :], axis=1, keepdims=True) * scale
        top = jnp.maximum(jnp.max(scores, axis=1, keepdims=True), own)
        prob = jnp.exp(scores - top)
        own_prob = jnp.exp(own - top)
        totals.append(jnp.sum(prob, axis=1, keepdims=True) + own_prob)
        own_weights.append(own_prob.astype(jnp.bfloat16).astype(jnp.float32))
        weights[s] = prob.astype(jnp.bfloat16)

    pl.semaphore_wait(barrier, BATCH - 1 + TENSOR - 1)

    def send_rows(step, carry):
        other = (member + step) & 7
        pltpu.make_async_remote_copy(
            src_ref=rows_hbm.at[0, :, pl.ds(pl.multiple_of(slice_of(other, tensor) * SLICE, 128), SLICE)],
            dst_ref=rows.at[member],
            send_sem=rows_send,
            recv_sem=rows_recv,
            device_id=(batch_of(clan * GROUP + other), tensor),
            device_id_type=MESH,
        ).start()
        return carry

    lax.fori_loop(1, GROUP, send_rows, 0)
    pltpu.make_async_copy(
        rows_hbm.at[0, :, pl.ds(pl.multiple_of(part * SLICE, 128), SLICE)],
        rows.at[member],
        rows_recv,
    ).start()

    for s in range(SEQS):
        pltpu.make_async_copy(values_hbm.at[s, 0], values.at[s], value_sem.at[s]).wait()
    for s in range(SEQS):
        mixed = lax.dot_general(
            weights[s], values[s], (((1,), (0,)), ((), ())), preferred_element_type=jnp.float32
        )
        mixed = (mixed + own_weights[s] * fresh_v[s : s + 1, :]) / totals[s]
        attended[s * HEADS : (s + 1) * HEADS, :] = mixed
        attended[(s + SEQS) * HEADS : (s + SEQS + 1) * HEADS, :] = mixed

    blocks = [jnp.zeros((8, 128), jnp.float32)] * CLANS
    for h in range(HEADS):
        head = attended[pl.ds(h, 8, stride=HEADS), :]
        for r in range(4):
            turned = pltpu.roll(head, r * PIECE, 1) if r else head
            goal = goals[h * 4 + r]
            blocks = [jnp.where(goal == c * GROUP, turned, blocks[c]) for c in range(CLANS)]
    for c in range(CLANS):
        message[c] = blocks[c].astype(jnp.bfloat16)

    def send_attended(step, carry):
        other = batch_at(batch, step)
        pltpu.make_async_remote_copy(
            src_ref=message.at[place_of(other) >> 3],
            dst_ref=gathered.at[batch],
            send_sem=att_send,
            recv_sem=att_recv,
            device_id=(other, tensor),
            device_id_type=MESH,
        ).start()
        return carry

    lax.fori_loop(0, BATCH - 1, send_attended, 0)
    pltpu.make_async_copy(message.at[clan], gathered.at[batch], att_recv).start()

    pltpu.make_async_copy(rows, rows, rows_recv).wait()
    pltpu.make_async_copy(gathered, gathered, att_recv).wait()

    first = gathered[...].astype(jnp.float32)
    swapped = pltpu.roll(first, SEQS, 1).reshape(BATCH * 8, 128).astype(jnp.bfloat16)
    first = first.reshape(BATCH * 8, 128).astype(jnp.bfloat16)
    table = rows[...].reshape(GROUP * PIECE, SLICE)
    product = jnp.dot(
        jnp.concatenate([first, swapped], axis=1), table, preferred_element_type=jnp.float32
    )
    partial[...] = product.reshape(BATCH, 8, SLICE)[:, :SEQS].astype(jnp.bfloat16)

    def send_partial(step, carry):
        other = batch_at(batch, step)
        local = mine & (step == BATCH - 1)

        @pl.when(jnp.logical_not(local))
        def _():
            pltpu.make_async_remote_copy(
                src_ref=partial.at[other],
                dst_ref=partials.at[tensor * CLANS + clan],
                send_sem=part_send,
                recv_sem=part_recv,
                device_id=(other, part),
                device_id_type=MESH,
            ).start()

        @pl.when(local)
        def _():
            pltpu.make_async_copy(
                partial.at[other], partials.at[tensor * CLANS + clan], part_recv
            ).start()

        return carry

    lax.fori_loop(0, BATCH, send_partial, 0)
    pltpu.make_async_copy(partials, partials, part_recv).wait()
    total = jnp.sum(partials[...].astype(jnp.float32), axis=0)
    stream = residual_ref[...].astype(jnp.float32) + total

    squared = jnp.sum(stream * stream, axis=1, keepdims=True)
    square[...] = jnp.broadcast_to(squared, (SEQS, 128))

    def send_square(step, carry):
        pltpu.make_async_remote_copy(
            src_ref=square,
            dst_ref=squares.at[step],
            send_sem=sq_send,
            recv_sem=sq_recv,
            device_id=(batch, tensor_at(tensor, step)),
            device_id_type=MESH,
        ).start()
        return carry

    lax.fori_loop(0, TENSOR - 1, send_square, 0)

    out_ref[0] = stream
    pltpu.make_async_copy(squares, squares, sq_recv).wait()
    mean = (squared + jnp.sum(squares[...], axis=0)[:, :1]) / D
    inverse = lax.rsqrt(mean + 1e-6)
    out_ref[1] = stream * inverse

    pltpu.make_async_copy(squares, squares, sq_send).wait()
    pltpu.make_async_copy(rows.at[: GROUP - 1], rows.at[: GROUP - 1], rows_send).wait()
    pltpu.make_async_copy(gathered.at[: BATCH - 1], gathered.at[: BATCH - 1], att_send).wait()
    pltpu.make_async_copy(partial.at[: BATCH - 1], partial.at[: BATCH - 1], part_send).wait()

    @pl.when(jnp.logical_not(mine))
    def _():
        pltpu.make_async_copy(partial.at[0], partial.at[0], part_send).wait()


def finish(x_ref, gain_ref, stream_ref, normed_ref):
    stream_ref[...] = x_ref[0].astype(jnp.bfloat16)
    gain = gain_ref[...].astype(jnp.float32).reshape(1, SLICE)
    normed_ref[...] = (x_ref[1] * gain).astype(jnp.bfloat16)


def local(
    queries,
    fresh_key_heads,
    fresh_value_heads,
    cached_keys,
    value_cache_rows,
    lengths,
    residual,
    sectioned_rows,
    owners,
    norm_gain,
):
    anywhere = pl.BlockSpec(memory_space=pl.ANY)
    bf16, f32 = jnp.bfloat16, jnp.float32
    out = pl.pallas_call(
        kernel,
        out_shape=pltpu.VMEM((2, SEQS, SLICE), f32),
        in_specs=[anywhere] * 9,
        out_specs=pl.BlockSpec(memory_space=pltpu.VMEM),
        scratch_shapes=[
            pltpu.VMEM((SEQS, HEADS * HEAD_SIZE), bf16),
            pltpu.VMEM((SEQS, HEAD_SIZE), bf16),
            pltpu.VMEM((SEQS, HEAD_SIZE), bf16),
            pltpu.SMEM((SEQS,), jnp.int32),
            pltpu.VMEM((SEQS, SLICE), bf16),
            pltpu.SMEM((BATCH,), jnp.int32),
            pltpu.VMEM((SEQS, SPAN, HEAD_SIZE), bf16),
            pltpu.VMEM((SEQS, SPAN, HEAD_SIZE), bf16),
            pltpu.VMEM((SEQS * HEADS, HEAD_SIZE), f32),
            pltpu.VMEM((SEQS, HEADS, SPAN), bf16),
            pltpu.VMEM((2 * SEQS * HEADS, HEAD_SIZE), f32),
            pltpu.VMEM((HEADS * 4, 8, 128), jnp.int32),
            pltpu.VMEM((CLANS, 8, 128), bf16),
            pltpu.VMEM((BATCH, 8, 128), bf16),
            pltpu.VMEM((GROUP, PIECE, SLICE), bf16),
            pltpu.VMEM((BATCH, SEQS, SLICE), bf16),
            pltpu.VMEM((BATCH, SEQS, SLICE), bf16),
            pltpu.VMEM((SEQS, 128), f32),
            pltpu.VMEM((TENSOR - 1, SEQS, 128), f32),
            pltpu.SemaphoreType.DMA((6,)),
            pltpu.SemaphoreType.DMA((SEQS,)),
            pltpu.SemaphoreType.DMA((SEQS,)),
        ]
        + [pltpu.SemaphoreType.DMA] * 8,
        compiler_params=pltpu.CompilerParams(
            collective_id=0, has_side_effects=True, vmem_limit_bytes=56 * 1024 * 1024
        ),
    )(
        queries,
        fresh_key_heads,
        fresh_value_heads,
        cached_keys,
        value_cache_rows,
        lengths,
        residual,
        sectioned_rows,
        owners,
    )
    block = jax.ShapeDtypeStruct((SEQS, SLICE), bf16)
    out = pltpu.with_memory_space_constraint(out, pltpu.VMEM)
    return pl.pallas_call(finish, out_shape=(block, block))(out, norm_gain)


def solution(mesh):
    return jax.shard_map(
        local,
        mesh=mesh,
        in_specs=(
            P("batch", "tensor"),
            P("batch", "tensor"),
            P("batch", "tensor"),
            P("batch", "tensor", None, None),
            P("batch", "tensor", None, None),
            P("batch"),
            P("batch", "tensor"),
            P("batch", "tensor", None),
            P(),
            P("tensor"),
        ),
        out_specs=(P("batch", "tensor"), P("batch", "tensor")),
        check_vma=False,
    )
```

time: 37.5 us -> 33.6 us (0.90)
  other arithmetic: 1.99 us -> 0 us
  local copies, waits for them, and re-layouts: 1.3 us -> 0 us
  Pallas kernels: 33.4 us -> 32.9 us
    convert_element_type x2 -> x0, other arithmetic: 1.99 us -> none  [local(): return (out[0].astype(bf16), (out[1] * norm_gain.astype(f32)).astype(bf16))]
    convert_element_type x1 -> x0, local copies, waits for them, and re-layouts: 1.3 us -> none  [local(): return (out[0].astype(bf16), (out[1] * norm_gain.astype(f32)).astype(bf16))]
    pallas_call x1 -> x2, Pallas kernels: 33.4 us -> 32.9 us  [the longest x1 31.6 us: local(): pl.pallas_call(kernel, out_shape=pltpu.VMEM((2, SEQS, SLICE), f32), in_sp...]
where the time goes in v3:
time: 33.6 us; the launch traced here: 33.5 us
  Pallas kernels  32.9 us (98%)
  between operations  0.64 us (2%)
    pallas_call x1, Pallas kernels, local(): pl.pallas_call(kernel, out_shape=pltpu.VMEM((2, SEQS, SLICE), f32), in_sp...  31.6 us
    pallas_call x1, Pallas kernels, local(): return pl.pallas_call(finish, out_shape=(block, block))(out, norm_gain)  1.29 us

profile of v3, /device:TPU:1, one launch (start us, length us, event | category | flops | bytes accessed | tf_op | source)
XLA Modules:
  0.0 33.5 jit_solution(3456263983055324508)
XLA Ops:
  0.6 31.6 %shard_map.113.x_ref = f32[2,4,640]{2,1,0:T(4,128)S(1)} custom-call(bf16[4,1024]{1,0:T(4,128)(2,1)} %q_hbm.1, bf16[4,128]{1,0:T(4,128)(2,1)} %fresh_k_hbm.1, bf16[4,128]{1,0:T(4,128)(2,1)} %fresh_v_hbm.1, bf16[4,1,4096,128]{3,2,1,0:T(8,128)(2,1)} %keys_hbm.1, bf16[4,1,4096,128]{3,2,1,0:T(8,128)(2,1)} %values_hbm.1, s32[4]{0:T(128)} %lengths_hbm.1, ...), custom_call_target="tpu_custom_call" | custom-call | tf_op jit(solution)/shard_map/pallas_call | solution.py:329
  32.2 1.3 %shard_map.114 = (bf16[4,640]{1,0:T(4,128)(2,1)}, bf16[4,640]{1,0:T(4,128)(2,1)}) custom-call(f32[2,4,640]{2,1,0:T(4,128)S(1)} %shard_map.113.x_ref, bf16[640]{0:T(1024)(128)(2,1)} %gain_ref.1), custom_call_target="tpu_custom_call" | custom-call | tf_op jit(solution)/shard_map/pallas_call | solution.py:375

commit v4 on v3

--- a/solution.py
+++ b/solution.py
@@ -16,6 +16,7 @@
 TENSOR = 8
 GROUP = 8
 CLANS = BATCH // GROUP
+PART = BATCH // 4
 PIECE = 32
 SLICE = D // TENSOR
 MESH = pl.DeviceIdType.MESH
@@ -44,6 +45,14 @@
     ring = step >> 1
     away = 2 + ((ring + 1) >> 1) * (1 - 2 * (ring & 1))
     return ((tensor + 2 * away) & 7) ^ (1 - (step & 1))
+
+
+def slot_of(batch):
+    return ((batch & 14) << 1) + ((batch >> 4) << 1) + (batch & 1)
+
+
+def batch_of_slot(slot):
+    return ((slot >> 1 & 1) << 4) + ((slot >> 2) << 1) + (slot & 1)
 
 
 def kernel(
@@ -93,6 +102,7 @@
     clan, member = place >> 3, place & 7
     part = slice_of(member, tensor)
     mine = part == tensor
+    late = (batch & 8) != 0
 
     small = [
         pltpu.make_async_copy(source, target, small_sem.at[i])
@@ -133,6 +143,30 @@
     lax.fori_loop(0, TENSOR - 1, greet_tensor, 0)
     lax.fori_loop(4, BATCH - 1, greet_batch, 0)
 
+    def send_rows(step, carry):
+        other = (member + step) & 7
+        pltpu.make_async_remote_copy(
+            src_ref=rows_hbm.at[0, :, pl.ds(pl.multiple_of(slice_of(other, tensor) * SLICE, 128), SLICE)],
+            dst_ref=rows.at[member],
+            send_sem=rows_send,
+            recv_sem=rows_recv,
+            device_id=(batch_of(clan * GROUP + other), tensor),
+            device_id_type=MESH,
+        ).start()
+        return carry
+
+    def open_up():
+        pl.semaphore_wait(barrier, BATCH - 1 + TENSOR - 1)
+
+    def recut():
+        lax.fori_loop(1, GROUP, send_rows, 0)
+        pltpu.make_async_copy(
+            rows_hbm.at[0, :, pl.ds(pl.multiple_of(part * SLICE, 128), SLICE)],
+            rows.at[member],
+            rows_recv,
+        ).start()
+
+
     for copy in small:
         copy.wait()
 
@@ -155,10 +189,17 @@
     fresh_v = fresh_v_ref[...].astype(jnp.float32)
     scale = HEAD_SIZE ** (-0.5)
     position = lax.broadcasted_iota(jnp.int32, (HEADS, SPAN), 1)
-    for s in range(SEQS):
-        pltpu.make_async_copy(keys_hbm.at[s, 0], keys.at[s], key_sem.at[s]).wait()
     own_weights, totals = [], []
     for s in range(SEQS):
+        if s == 2:
+            @pl.when(late)
+            def _():
+                open_up()
+                recut()
+
+        if s % 2 == 0:
+            for r in range(s, s + 2):
+                pltpu.make_async_copy(keys_hbm.at[r, 0], keys.at[r], key_sem.at[r]).wait()
         q = q_by_head[s * HEADS : (s + 1) * HEADS, :]
         scores = (
             lax.dot_general(
@@ -178,27 +219,6 @@
         own_weights.append(own_prob.astype(jnp.bfloat16).astype(jnp.float32))
         weights[s] = prob.astype(jnp.bfloat16)
 
-    pl.semaphore_wait(barrier, BATCH - 1 + TENSOR - 1)
-
-    def send_rows(step, carry):
-        other = (member + step) & 7
-        pltpu.make_async_remote_copy(
-            src_ref=rows_hbm.at[0, :, pl.ds(pl.multiple_of(slice_of(other, tensor) * SLICE, 128), SLICE)],
-            dst_ref=rows.at[member],
-            send_sem=rows_send,
-            recv_sem=rows_recv,
-            device_id=(batch_of(clan * GROUP + other), tensor),
-            device_id_type=MESH,
-        ).start()
-        return carry
-
-    lax.fori_loop(1, GROUP, send_rows, 0)
-    pltpu.make_async_copy(
-        rows_hbm.at[0, :, pl.ds(pl.multiple_of(part * SLICE, 128), SLICE)],
-        rows.at[member],
-        rows_recv,
-    ).start()
-
     for s in range(SEQS):
         pltpu.make_async_copy(values_hbm.at[s, 0], values.at[s], value_sem.at[s]).wait()
     for s in range(SEQS):
@@ -219,57 +239,75 @@
     for c in range(CLANS):
         message[c] = blocks[c].astype(jnp.bfloat16)
 
+    slot = slot_of(batch)
+    chunk = slot // PART
+
     def send_attended(step, carry):
         other = batch_at(batch, step)
         pltpu.make_async_remote_copy(
             src_ref=message.at[place_of(other) >> 3],
-            dst_ref=gathered.at[batch],
+            dst_ref=gathered.at[slot],
             send_sem=att_send,
-            recv_sem=att_recv,
+            recv_sem=att_recv.at[chunk],
             device_id=(other, tensor),
             device_id_type=MESH,
         ).start()
         return carry
 
+    @pl.when(jnp.logical_not(late))
+    def _():
+        open_up()
+
     lax.fori_loop(0, BATCH - 1, send_attended, 0)
-    pltpu.make_async_copy(message.at[clan], gathered.at[batch], att_recv).start()
+    pltpu.make_async_copy(message.at[clan], gathered.at[slot], att_recv.at[chunk]).start()
+
+    @pl.when(jnp.logical_not(late))
+    def _():
+        recut()
+
 
     pltpu.make_async_copy(rows, rows, rows_recv).wait()
-    pltpu.make_async_copy(gathered, gathered, att_recv).wait()
-
-    first = gathered[...].astype(jnp.float32)
-    swapped = pltpu.roll(first, SEQS, 1).reshape(BATCH * 8, 128).astype(jnp.bfloat16)
-    first = first.reshape(BATCH * 8, 128).astype(jnp.bfloat16)
-    table = rows[...].reshape(GROUP * PIECE, SLICE)
-    product = jnp.dot(
-        jnp.concatenate([first, swapped], axis=1), table, preferred_element_type=jnp.float32
-    )
-    partial[...] = product.reshape(BATCH, 8, SLICE)[:, :SEQS].astype(jnp.bfloat16)
-
-    def send_partial(step, carry):
-        other = batch_at(batch, step)
-        local = mine & (step == BATCH - 1)
-
-        @pl.when(jnp.logical_not(local))
-        def _():
-            pltpu.make_async_remote_copy(
-                src_ref=partial.at[other],
-                dst_ref=partials.at[tensor * CLANS + clan],
-                send_sem=part_send,
-                recv_sem=part_recv,
-                device_id=(other, part),
-                device_id_type=MESH,
-            ).start()
-
-        @pl.when(local)
-        def _():
-            pltpu.make_async_copy(
-                partial.at[other], partials.at[tensor * CLANS + clan], part_recv
-            ).start()
-
-        return carry
-
-    lax.fori_loop(0, BATCH, send_partial, 0)
+
+
+    def project(turn, carry):
+        table = rows[...].reshape(GROUP * PIECE, SLICE)
+        here = pl.ds(turn * PART, PART)
+        pltpu.make_async_copy(gathered.at[here], gathered.at[here], att_recv.at[turn]).wait()
+        first = gathered[here].astype(jnp.float32)
+        swapped = pltpu.roll(first, SEQS, 1).reshape(PART * 8, 128).astype(jnp.bfloat16)
+        first = first.reshape(PART * 8, 128).astype(jnp.bfloat16)
+        product = jnp.dot(
+            jnp.concatenate([first, swapped], axis=1), table, preferred_element_type=jnp.float32
+        )
+        partial[here] = product.reshape(PART, 8, SLICE)[:, :SEQS].astype(jnp.bfloat16)
+
+        def send_partial(step, carry):
+            other = turn * PART + step
+            local = mine & (other == slot)
+
+            @pl.when(jnp.logical_not(local))
+            def _():
+                pltpu.make_async_remote_copy(
+                    src_ref=partial.at[other],
+                    dst_ref=partials.at[tensor * CLANS + clan],
+                    send_sem=part_send,
+                    recv_sem=part_recv,
+                    device_id=(batch_of_slot(other), part),
+                    device_id_type=MESH,
+                ).start()
+
+            @pl.when(local)
+            def _():
+                pltpu.make_async_copy(
+                    partial.at[other], partials.at[tensor * CLANS + clan], part_recv
+                ).start()
+
+            return carry
+
+        lax.fori_loop(0, PART, send_partial, 0)
+        return carry
+
+    lax.fori_loop(0, BATCH // PART, project, 0)
     pltpu.make_async_copy(partials, partials, part_recv).wait()
     total = jnp.sum(partials[...].astype(jnp.float32), axis=0)
     stream = residual_ref[...].astype(jnp.float32) + total
@@ -355,7 +393,9 @@
             pltpu.SemaphoreType.DMA((SEQS,)),
             pltpu.SemaphoreType.DMA((SEQS,)),
         ]
-        + [pltpu.SemaphoreType.DMA] * 8,
+        + [pltpu.SemaphoreType.DMA] * 3
+        + [pltpu.SemaphoreType.DMA((BATCH // PART,))]
+        + [pltpu.SemaphoreType.DMA] * 4,
         compiler_params=pltpu.CompilerParams(
             collective_id=0, has_side_effects=True, vmem_limit_bytes=56 * 1024 * 1024
         ),

time: 33.6 us -> 30.5 us (0.908)
  Pallas kernels: 32.9 us -> 29.7 us
    pallas_call x1, Pallas kernels: 31.6 us -> 28.4 us  [local(): pl.pallas_call(kernel, out_shape=pltpu.VMEM((2, SEQS, SLICE), f32), in_sp...]
where the time goes in v4:
time: 30.5 us; the launch traced here: 30.3 us
  Pallas kernels  29.7 us (97%)
  between operations  0.64 us (2%)
    pallas_call x1, Pallas kernels, local(): pl.pallas_call(kernel, out_shape=pltpu.VMEM((2, SEQS, SLICE), f32), in_sp...  28.4 us
    pallas_call x1, Pallas kernels, local(): return pl.pallas_call(finish, out_shape=(block, block))(out, norm_gain)  1.29 us

profile of v4, /device:TPU:1, one launch (start us, length us, event | category | flops | bytes accessed | tf_op | source)
XLA Modules:
  0.0 30.3 jit_solution(3967574617304878659)
XLA Ops:
  0.6 28.4 %shard_map.113.x_ref = f32[2,4,640]{2,1,0:T(4,128)S(1)} custom-call(bf16[4,1024]{1,0:T(4,128)(2,1)} %q_hbm.1, bf16[4,128]{1,0:T(4,128)(2,1)} %fresh_k_hbm.1, bf16[4,128]{1,0:T(4,128)(2,1)} %fresh_v_hbm.1, bf16[4,1,4096,128]{3,2,1,0:T(8,128)(2,1)} %keys_hbm.1, bf16[4,1,4096,128]{3,2,1,0:T(8,128)(2,1)} %values_hbm.1, s32[4]{0:T(128)} %lengths_hbm.1, ...), custom_call_target="tpu_custom_call" | custom-call | tf_op jit(solution)/shard_map/pallas_call | solution.py:367
  29.0 1.3 %shard_map.114 = (bf16[4,640]{1,0:T(4,128)(2,1)}, bf16[4,640]{1,0:T(4,128)(2,1)}) custom-call(f32[2,4,640]{2,1,0:T(4,128)S(1)} %shard_map.113.x_ref, bf16[640]{0:T(1024)(128)(2,1)} %gain_ref.1), custom_call_target="tpu_custom_call" | custom-call | tf_op jit(solution)/shard_map/pallas_call | solution.py:415

commit v5 on v4

--- a/solution.py
+++ b/solution.py
@@ -19,6 +19,7 @@
 PART = BATCH // 4
 PIECE = 32
 SLICE = D // TENSOR
+RECUT_ORDER = 0x1246357
 MESH = pl.DeviceIdType.MESH
 
 
@@ -65,13 +66,16 @@
     residual_hbm,
     rows_hbm,
     owners_hbm,
-    out_ref,
+    gain_hbm,
+    stream_ref,
+    normed_ref,
     q_ref,
     fresh_k_ref,
     fresh_v_ref,
     lengths_ref,
     residual_ref,
     owners_ref,
+    gain_ref,
     keys,
     values,
     q_by_head,
@@ -112,8 +116,9 @@
                 (fresh_k_hbm, fresh_k_ref),
                 (fresh_v_hbm, fresh_v_ref),
                 (lengths_hbm, lengths_ref),
+                (owners_hbm, owners_ref),
                 (residual_hbm, residual_ref),
-                (owners_hbm, owners_ref),
+                (gain_hbm, gain_ref),
             )
         )
     ]
@@ -144,7 +149,7 @@
     lax.fori_loop(4, BATCH - 1, greet_batch, 0)
 
     def send_rows(step, carry):
-        other = (member + step) & 7
+        other = member ^ (RECUT_ORDER >> 4 * (step - 1) & 7)
         pltpu.make_async_remote_copy(
             src_ref=rows_hbm.at[0, :, pl.ds(pl.multiple_of(slice_of(other, tensor) * SLICE, 128), SLICE)],
             dst_ref=rows.at[member],
@@ -167,7 +172,7 @@
         ).start()
 
 
-    for copy in small:
+    for copy in small[:5]:
         copy.wait()
 
     row = lax.broadcasted_iota(jnp.int32, (8, 128), 0)
@@ -308,6 +313,8 @@
         return carry
 
     lax.fori_loop(0, BATCH // PART, project, 0)
+    for copy in small[5:]:
+        copy.wait()
     pltpu.make_async_copy(partials, partials, part_recv).wait()
     total = jnp.sum(partials[...].astype(jnp.float32), axis=0)
     stream = residual_ref[...].astype(jnp.float32) + total
@@ -328,11 +335,12 @@
 
     lax.fori_loop(0, TENSOR - 1, send_square, 0)
 
-    out_ref[0] = stream
+    stream_ref[...] = stream.astype(jnp.bfloat16)
+    scaled = stream * gain_ref[...].astype(jnp.float32).reshape(1, SLICE)
     pltpu.make_async_copy(squares, squares, sq_recv).wait()
     mean = (squared + jnp.sum(squares[...], axis=0)[:, :1]) / D
     inverse = lax.rsqrt(mean + 1e-6)
-    out_ref[1] = stream * inverse
+    normed_ref[...] = (scaled * inverse).astype(jnp.bfloat16)
 
     pltpu.make_async_copy(squares, squares, sq_send).wait()
     pltpu.make_async_copy(rows.at[: GROUP - 1], rows.at[: GROUP - 1], rows_send).wait()
@@ -344,10 +352,15 @@
         pltpu.make_async_copy(partial.at[0], partial.at[0], part_send).wait()
 
 
-def finish(x_ref, gain_ref, stream_ref, normed_ref):
-    stream_ref[...] = x_ref[0].astype(jnp.bfloat16)
-    gain = gain_ref[...].astype(jnp.float32).reshape(1, SLICE)
-    normed_ref[...] = (x_ref[1] * gain).astype(jnp.bfloat16)
+def finish(stream_ref, normed_ref, stream_hbm, normed_hbm, sem):
+    copies = [
+        pltpu.make_async_copy(stream_ref, stream_hbm, sem.at[0]),
+        pltpu.make_async_copy(normed_ref, normed_hbm, sem.at[1]),
+    ]
+    for copy in copies:
+        copy.start()
+    for copy in copies:
+        copy.wait()
 
 
 def local(
@@ -364,11 +377,11 @@
 ):
     anywhere = pl.BlockSpec(memory_space=pl.ANY)
     bf16, f32 = jnp.bfloat16, jnp.float32
-    out = pl.pallas_call(
+    outs = pl.pallas_call(
         kernel,
-        out_shape=pltpu.VMEM((2, SEQS, SLICE), f32),
-        in_specs=[anywhere] * 9,
-        out_specs=pl.BlockSpec(memory_space=pltpu.VMEM),
+        out_shape=(pltpu.VMEM((SEQS, SLICE), bf16),) * 2,
+        in_specs=[anywhere] * 10,
+        out_specs=(pl.BlockSpec(memory_space=pltpu.VMEM),) * 2,
         scratch_shapes=[
             pltpu.VMEM((SEQS, HEADS * HEAD_SIZE), bf16),
             pltpu.VMEM((SEQS, HEAD_SIZE), bf16),
@@ -376,6 +389,7 @@
             pltpu.SMEM((SEQS,), jnp.int32),
             pltpu.VMEM((SEQS, SLICE), bf16),
             pltpu.SMEM((BATCH,), jnp.int32),
+            pltpu.VMEM((SLICE,), bf16),
             pltpu.VMEM((SEQS, SPAN, HEAD_SIZE), bf16),
             pltpu.VMEM((SEQS, SPAN, HEAD_SIZE), bf16),
             pltpu.VMEM((SEQS * HEADS, HEAD_SIZE), f32),
@@ -389,7 +403,7 @@
             pltpu.VMEM((BATCH, SEQS, SLICE), bf16),
             pltpu.VMEM((SEQS, 128), f32),
             pltpu.VMEM((TENSOR - 1, SEQS, 128), f32),
-            pltpu.SemaphoreType.DMA((6,)),
+            pltpu.SemaphoreType.DMA((7,)),
             pltpu.SemaphoreType.DMA((SEQS,)),
             pltpu.SemaphoreType.DMA((SEQS,)),
         ]
@@ -409,10 +423,17 @@
         residual,
         sectioned_rows,
         owners,
+        norm_gain,
     )
     block = jax.ShapeDtypeStruct((SEQS, SLICE), bf16)
-    out = pltpu.with_memory_space_constraint(out, pltpu.VMEM)
-    return pl.pallas_call(finish, out_shape=(block, block))(out, norm_gain)
+    return pl.pallas_call(
+        finish,
+        out_shape=(block, block),
+        in_specs=[pl.BlockSpec(memory_space=pltpu.VMEM)] * 2,
+        out_specs=(anywhere, anywhere),
+        scratch_shapes=[pltpu.SemaphoreType.DMA((2,))],
+    )(*[pltpu.with_memory_space_constraint(x, pltpu.VMEM) for x in outs])
+    block = jax.ShapeDtypeStruct((SEQS, SLICE), bf16)
 
 
 def solution(mesh):

time: 30.5 us -> 28.8 us (0.944)
  Pallas kernels: 29.7 us -> 28 us
    pallas_call x2, Pallas kernels: 29.7 us -> 28 us  [the longest x1 27.4 us: local(): pl.pallas_call(kernel, out_shape=(pltpu.VMEM((SEQS, SLICE), bf16),) * 2,...]
where the time goes in v5:
time: 28.8 us; the launch traced here: 28.7 us
  Pallas kernels  28 us (97%)
  between operations  0.64 us (2%)
    pallas_call x1, Pallas kernels, local(): pl.pallas_call(kernel, out_shape=(pltpu.VMEM((SEQS, SLICE), bf16),) * 2,...  27.4 us
    pallas_call x1, Pallas kernels, local(): pl.pallas_call(finish, out_shape=(block, block), in_specs=[pl.BlockSpec(m...  0.62 us

profile of v5, /device:TPU:1, one launch (start us, length us, event | category | flops | bytes accessed | tf_op | source)
XLA Modules:
  0.0 28.7 jit_solution(1310646345879797028)
XLA Ops:
  0.6 27.4 %shard_map.113 = (bf16[4,640]{1,0:T(4,128)(2,1)S(1)}, bf16[4,640]{1,0:T(4,128)(2,1)S(1)}) custom-call(bf16[4,1024]{1,0:T(4,128)(2,1)} %q_hbm.1, bf16[4,128]{1,0:T(4,128)(2,1)} %fresh_k_hbm.1, bf16[4,128]{1,0:T(4,128)(2,1)} %fresh_v_hbm.1, bf16[4,1,4096,128]{3,2,1,0:T(8,128)(2,1)} %keys_hbm.1, bf16[4,1,4096,128]{3,2,1,0:T(8,128)(2,1)} %values_hbm.1, ...), custom_call_target="tpu_custom_call" | custom-call | tf_op jit(solution)/shard_map/pallas_call | solution.py:380
  28.1 0.6 %shard_map.114 = (bf16[4,640]{1,0:T(4,128)(2,1)}, bf16[4,640]{1,0:T(4,128)(2,1)}) custom-call(bf16[4,640]{1,0:T(4,128)(2,1)S(1)} %get-tuple-element.4.stream_ref, bf16[4,640]{1,0:T(4,128)(2,1)S(1)} %get-tuple-element.5.normed_ref), custom_call_target="tpu_custom_call" | custom-call | tf_op jit(solution)/shard_map/pallas_call | solution.py:429

commit v6 on v5

--- a/solution.py
+++ b/solution.py
@@ -19,7 +19,7 @@
 PART = BATCH // 4
 PIECE = 32
 SLICE = D // TENSOR
-RECUT_ORDER = 0x1246357
+RECUT_ORDER = 0x2461357
 MESH = pl.DeviceIdType.MESH
 
 
@@ -32,8 +32,8 @@
 
 
 def slice_of(member, tensor):
-    step = 2 * (member & 1) + ((member >> 2) ^ (member >> 1 & 1))
-    return ((tensor + 2 * step) & 7) ^ (member >> 1 & 1)
+    step = 2 * (member & 1) + (member >> 1 & 1)
+    return ((tensor + 2 * step) & 7) ^ (member >> 2)
 
 
 def batch_at(batch, step):
@@ -84,12 +84,14 @@
     goals,
     message,
     gathered,
+    staged,
     rows,
     partial,
     partials,
     square,
     squares,
     small_sem,
+    staged_sem,
     key_sem,
     value_sem,
     rows_send,
@@ -126,6 +128,7 @@
         copy.start()
     for s in range(SEQS):
         pltpu.make_async_copy(keys_hbm.at[s, 0], keys.at[s], key_sem.at[s]).start()
+    pltpu.make_async_copy(rows_hbm.at[0], staged, staged_sem).start()
     for s in range(SEQS):
         pltpu.make_async_copy(values_hbm.at[s, 0], values.at[s], value_sem.at[s]).start()
 
@@ -151,7 +154,7 @@
     def send_rows(step, carry):
         other = member ^ (RECUT_ORDER >> 4 * (step - 1) & 7)
         pltpu.make_async_remote_copy(
-            src_ref=rows_hbm.at[0, :, pl.ds(pl.multiple_of(slice_of(other, tensor) * SLICE, 128), SLICE)],
+            src_ref=staged.at[:, pl.ds(pl.multiple_of(slice_of(other, tensor) * SLICE, 128), SLICE)],
             dst_ref=rows.at[member],
             send_sem=rows_send,
             recv_sem=rows_recv,
@@ -164,9 +167,10 @@
         pl.semaphore_wait(barrier, BATCH - 1 + TENSOR - 1)
 
     def recut():
+        pltpu.make_async_copy(rows_hbm.at[0], staged, staged_sem).wait()
         lax.fori_loop(1, GROUP, send_rows, 0)
         pltpu.make_async_copy(
-            rows_hbm.at[0, :, pl.ds(pl.multiple_of(part * SLICE, 128), SLICE)],
+            staged.at[:, pl.ds(pl.multiple_of(part * SLICE, 128), SLICE)],
             rows.at[member],
             rows_recv,
         ).start()
@@ -398,12 +402,14 @@
             pltpu.VMEM((HEADS * 4, 8, 128), jnp.int32),
             pltpu.VMEM((CLANS, 8, 128), bf16),
             pltpu.VMEM((BATCH, 8, 128), bf16),
+            pltpu.VMEM((PIECE, D), bf16),
             pltpu.VMEM((GROUP, PIECE, SLICE), bf16),
             pltpu.VMEM((BATCH, SEQS, SLICE), bf16),
             pltpu.VMEM((BATCH, SEQS, SLICE), bf16),
             pltpu.VMEM((SEQS, 128), f32),
             pltpu.VMEM((TENSOR - 1, SEQS, 128), f32),
             pltpu.SemaphoreType.DMA((7,)),
+            pltpu.SemaphoreType.DMA,
             pltpu.SemaphoreType.DMA((SEQS,)),
             pltpu.SemaphoreType.DMA((SEQS,)),
         ]

time: 28.8 us -> 28.2 us (0.979)
  Pallas kernels: 28 us -> 27.4 us
    pallas_call x1, Pallas kernels: 27.4 us -> 26.8 us  [local(): pl.pallas_call(kernel, out_shape=(pltpu.VMEM((SEQS, SLICE), bf16),) * 2,...]
where the time goes in v6:
time: 28.2 us; the launch traced here: 28.1 us
  Pallas kernels  27.4 us (97%)
  between operations  0.64 us (2%)
    pallas_call x1, Pallas kernels, local(): pl.pallas_call(kernel, out_shape=(pltpu.VMEM((SEQS, SLICE), bf16),) * 2,...  26.8 us
    pallas_call x1, Pallas kernels, local(): pl.pallas_call(finish, out_shape=(block, block), in_specs=[pl.BlockSpec(m...  0.62 us

profile of v6, /device:TPU:1, one launch (start us, length us, event | category | flops | bytes accessed | tf_op | source)
XLA Modules:
  0.0 28.1 jit_solution(15427014529238069123)
XLA Ops:
  0.6 26.8 %shard_map.113 = (bf16[4,640]{1,0:T(4,128)(2,1)S(1)}, bf16[4,640]{1,0:T(4,128)(2,1)S(1)}) custom-call(bf16[4,1024]{1,0:T(4,128)(2,1)} %q_hbm.1, bf16[4,128]{1,0:T(4,128)(2,1)} %fresh_k_hbm.1, bf16[4,128]{1,0:T(4,128)(2,1)} %fresh_v_hbm.1, bf16[4,1,4096,128]{3,2,1,0:T(8,128)(2,1)} %keys_hbm.1, bf16[4,1,4096,128]{3,2,1,0:T(8,128)(2,1)} %values_hbm.1, ...), custom_call_target="tpu_custom_call" | custom-call | tf_op jit(solution)/shard_map/pallas_call | solution.py:384
  27.5 0.6 %shard_map.114 = (bf16[4,640]{1,0:T(4,128)(2,1)}, bf16[4,640]{1,0:T(4,128)(2,1)}) custom-call(bf16[4,640]{1,0:T(4,128)(2,1)S(1)} %get-tuple-element.4.stream_ref, bf16[4,640]{1,0:T(4,128)(2,1)S(1)} %get-tuple-element.5.normed_ref), custom_call_target="tpu_custom_call" | custom-call | tf_op jit(solution)/shard_map/pallas_call | solution.py:435

commit v7 on v6

--- a/solution.py
+++ b/solution.py
@@ -19,7 +19,7 @@
 PART = BATCH // 4
 PIECE = 32
 SLICE = D // TENSOR
-RECUT_ORDER = 0x2461357
+RECUT_ORDER = 0x4261537
 MESH = pl.DeviceIdType.MESH
 
 
@@ -38,7 +38,8 @@
 
 def batch_at(batch, step):
     ring, rest = step >> 2, 3 - (step & 3)
-    away = 4 + ((ring + 1) >> 1) * (1 - 2 * (ring & 1))
+    side = 1 - 2 * (batch & 1)
+    away = 4 + side * ((ring + 1) >> 1) * (1 - 2 * (ring & 1))
     return ((batch & 16) ^ ((rest & 2) << 3)) + ((((batch & 15) + 2 * away) & 15) ^ (rest & 1))
 
 
@@ -341,19 +342,20 @@
 
     stream_ref[...] = stream.astype(jnp.bfloat16)
     scaled = stream * gain_ref[...].astype(jnp.float32).reshape(1, SLICE)
+    pltpu.make_async_copy(rows.at[: GROUP - 1], rows.at[: GROUP - 1], rows_send).wait()
+    pltpu.make_async_copy(gathered.at[: BATCH - 1], gathered.at[: BATCH - 1], att_send).wait()
+    pltpu.make_async_copy(partial.at[: BATCH - 1], partial.at[: BATCH - 1], part_send).wait()
+
+    @pl.when(jnp.logical_not(mine))
+    def _():
+        pltpu.make_async_copy(partial.at[0], partial.at[0], part_send).wait()
+
     pltpu.make_async_copy(squares, squares, sq_recv).wait()
     mean = (squared + jnp.sum(squares[...], axis=0)[:, :1]) / D
     inverse = lax.rsqrt(mean + 1e-6)
     normed_ref[...] = (scaled * inverse).astype(jnp.bfloat16)
 
     pltpu.make_async_copy(squares, squares, sq_send).wait()
-    pltpu.make_async_copy(rows.at[: GROUP - 1], rows.at[: GROUP - 1], rows_send).wait()
-    pltpu.make_async_copy(gathered.at[: BATCH - 1], gathered.at[: BATCH - 1], att_send).wait()
-    pltpu.make_async_copy(partial.at[: BATCH - 1], partial.at[: BATCH - 1], part_send).wait()
-
-    @pl.when(jnp.logical_not(mine))
-    def _():
-        pltpu.make_async_copy(partial.at[0], partial.at[0], part_send).wait()
 
 
 def finish(stream_ref, normed_ref, stream_hbm, normed_hbm, sem):

time: 28.2 us -> 28.2 us (level)
  no operation moved by 1% of the time
where the time goes in v7:
time: 28.2 us; the launch traced here: 28.1 us
  Pallas kernels  27.4 us (97%)
  between operations  0.64 us (2%)
    pallas_call x1, Pallas kernels, local(): pl.pallas_call(kernel, out_shape=(pltpu.VMEM((SEQS, SLICE), bf16),) * 2,...  26.8 us
    pallas_call x1, Pallas kernels, local(): pl.pallas_call(finish, out_shape=(block, block), in_specs=[pl.BlockSpec(m...  0.62 us

profile of v7, /device:TPU:1, one launch (start us, length us, event | category | flops | bytes accessed | tf_op | source)
XLA Modules:
  0.0 28.1 jit_solution(2499249331886464625)
XLA Ops:
  0.6 26.8 %shard_map.113 = (bf16[4,640]{1,0:T(4,128)(2,1)S(1)}, bf16[4,640]{1,0:T(4,128)(2,1)S(1)}) custom-call(bf16[4,1024]{1,0:T(4,128)(2,1)} %q_hbm.1, bf16[4,128]{1,0:T(4,128)(2,1)} %fresh_k_hbm.1, bf16[4,128]{1,0:T(4,128)(2,1)} %fresh_v_hbm.1, bf16[4,1,4096,128]{3,2,1,0:T(8,128)(2,1)} %keys_hbm.1, bf16[4,1,4096,128]{3,2,1,0:T(8,128)(2,1)} %values_hbm.1, ...), custom_call_target="tpu_custom_call" | custom-call | tf_op jit(solution)/shard_map/pallas_call | solution.py:386
  27.5 0.6 %shard_map.114 = (bf16[4,640]{1,0:T(4,128)(2,1)}, bf16[4,640]{1,0:T(4,128)(2,1)}) custom-call(bf16[4,640]{1,0:T(4,128)(2,1)S(1)} %get-tuple-element.4.stream_ref, bf16[4,640]{1,0:T(4,128)(2,1)S(1)} %get-tuple-element.5.normed_ref), custom_call_target="tpu_custom_call" | custom-call | tf_op jit(solution)/shard_map/pallas_call | solution.py:437
